TPU v7x, 32 devices: a whole 2x2x4 slice. The times are simulated.
32 devices in a mesh: grp: 4 (over y, x), cell: 8 (over z, core).
Axes of the slice: x: 2, y: 2, z: 4, core: 2. Of those that a mesh axis runs over, the one named last changes fastest.
Arguments:
- occurrence: bfloat16 [98304, 4096], P(('grp', 'cell')), may hold values from 0 to 1, as said below
- condition: bfloat16 [98304], P(('grp', 'cell')), may hold values from 0.05 to 1, as said below
- neighbours: int32 [768, 4], P(('grp', 'cell')), may hold values from 0 to 767, as said below
- pair_count: int32 [768], P(('grp', 'cell')), may hold values from 0 to 4
Outputs:
- effective: float32 [98304], P(('grp', 'cell'))
- persistence: float32 [4096], P(('grp', 'cell'))
Inputs may be any that keep to these rules, and one draw needn't show every extreme that they name: occurrence probabilities, positive. habitat condition, positive. `neighbours`: entry k of row t, for k < pair_count[t], is a tile u != t with |u - t| <= 2 in the same band of 192 consecutive tiles (t // 192 == u // 192); entries are distinct; pairing is symmetric (u lists t whenever t lists u); later entries hold t.
All inputs are finite; a program needn't handle non-finite values.
Results may differ from a plain program's by a relative error of at most 0.0003.
Values may be sent and summed in bfloat16 or wider, within the bound.
A program may use at most 384 MiB of HBM per device.

v0:
```python
import jax
import jax.numpy as jnp
from jax import lax
from jax.sharding import PartitionSpec as P

sharpness = 40.0
epsilon = 1e-06
exponent = 0.25


def extended_2(cells, sides, width):
    for axis, dim in sides:
        count = lax.axis_size(axis)
        ends = count - 1
        head = lax.slice_in_dim(cells, 0, width, axis=dim)
        tail = lax.slice_in_dim(cells, cells.shape[dim] - width, cells.shape[dim], axis=dim)
        cells = jnp.concatenate(
            [
                lax.ppermute(tail, axis, [(i, (i + 1) % count) for i in range(ends)]),
                cells,
                lax.ppermute(head, axis, [((i + 1) % count, i) for i in range(ends)]),
            ],
            axis=dim,
        )
    return cells


def pair_hits(neighbours, counts, first_tile, radius):
    own_tiles = first_tile + jnp.arange(counts.shape[0], dtype=jnp.int32)
    live_slot = jnp.arange(neighbours.shape[1], dtype=jnp.int32)[None, :] < counts[:, None]
    offsets = jnp.arange(-radius, radius + 1, dtype=jnp.int32)
    hit_tile = (neighbours - own_tiles[:, None])[:, :, None] == offsets[None, None, :]
    matched = jnp.any(live_slot[:, :, None] & hit_tile, axis=1) | (offsets == 0)[None, :]
    return matched.astype(jnp.float32)


def inverse_norms(block_rows):
    squares = jnp.einsum("cs,cs->c", block_rows, block_rows, preferred_element_type=jnp.float32)
    return lax.rsqrt(squares + epsilon)


def tile_terms(row_tiles, view_tiles, row_inv, view_inv, hit_column, self_pair):
    gram = jnp.einsum("tis,tjs->tij", row_tiles, view_tiles, preferred_element_type=jnp.float32)
    cosine = gram * row_inv[:, :, None] * view_inv[:, None, :]
    weights = jnp.exp(sharpness * cosine) * hit_column[:, None, None]
    if self_pair:
        diagonal = jnp.eye(row_tiles.shape[1], dtype=bool)
        weights = jnp.where(diagonal[None, :, :], 0.0, weights)
    return weights


def per_device(occurrence, condition, neighbours, pair_count):
    tiles_here = pair_count.shape[0]
    radius = neighbours.shape[1] // 2
    rows_here = occurrence.shape[0]
    tile_rows = rows_here // tiles_here
    species_all = occurrence.shape[1]
    rim_rows = radius * tile_rows
    first_tile = (
        lax.axis_index("grp") * lax.axis_size("cell") + lax.axis_index("cell")
    ) * tiles_here
    hits = pair_hits(neighbours, pair_count, first_tile, radius)
    cond_full = condition.astype(jnp.float32)
    row_tiles = occurrence.reshape(tiles_here, tile_rows, species_all)
    extended, ext_half = (
        extended_2(occurrence, (("cell", 0),), rim_rows),
        extended_2(condition, (("cell", 0),), rim_rows),
    )
    ext_tiles = extended.reshape(tiles_here + 2 * radius, tile_rows, species_all)
    ext_cond = ext_half.astype(jnp.float32).reshape(tiles_here + 2 * radius, tile_rows)
    ext_inv = inverse_norms(extended).reshape(tiles_here + 2 * radius, tile_rows)
    row_inv = ext_inv[radius : radius + tiles_here]
    numer = jnp.zeros((tiles_here, tile_rows), jnp.float32)
    denom = jnp.zeros((tiles_here, tile_rows), jnp.float32)
    for offset in range(2 * radius + 1):
        weights = tile_terms(
            row_tiles,
            ext_tiles[offset : offset + tiles_here],
            row_inv,
            ext_inv[offset : offset + tiles_here],
            hits[:, offset],
            offset == radius,
        )
        numer = numer + jnp.sum(
            weights * ext_cond[offset : offset + tiles_here][:, None, :], axis=2
        )
        denom = denom + jnp.sum(weights, axis=2)
    numer = numer.reshape(rows_here)
    denom = denom.reshape(rows_here)
    effective = cond_full * numer / denom
    weighted = jnp.stack([effective.astype(jnp.bfloat16), jnp.ones((rows_here,), jnp.bfloat16)])
    partial_sums = jnp.dot(weighted, occurrence, preferred_element_type=jnp.float32)
    totals = lax.psum_scatter(partial_sums, ("grp", "cell"), scatter_dimension=1, tiled=True)
    persistence = (totals[0] / totals[1]) ** exponent
    return (effective, persistence)


def solution(mesh):
    return jax.shard_map(
        per_device,
        mesh=mesh,
        in_specs=(
            P(("grp", "cell"), None),
            P(("grp", "cell")),
            P(("grp", "cell"), None),
            P(("grp", "cell")),
        ),
        out_specs=(P(("grp", "cell")), P(("grp", "cell"))),
        check_vma=False,
    )
```

profile of v0, /device:TPU:0, one launch (start us, length us, event | category | flops | bytes accessed | tf_op | source)
XLA Modules:
  0.0 410.8 jit_solution(5303702926150256437)
XLA Ops:
  7.2 0.0 copy-start
  7.2 0.0 copy-start.5
  7.2 0.0 copy-start.3
  7.2 0.0 reduce-scatter.4.cloned.1.call-start
  7.2 4.6 %fusion.10 = (bf16[256,4096]{1,0:T(8,128)(2,1)}, bf16[256,4096]{1,0:T(8,128)(2,1)}) fusion(bf16[3072,4096]{1,0:T(8,128)(2,1)} %param.4), kind=kLoop, calls=%fused_computation.58 | loop fusion | bytes 8388608 | tf_op jit(solution)/shard_map/slice | solution.py:16
  11.9 3.6 collective-permute-start
  15.5 1.3 collective-permute-start.1
  16.8 0.0 copy-done
  16.9 3.9 collective-permute-start.2
  20.8 1.3 collective-permute-start.3
  22.1 0.0 copy-done.5
  22.2 0.0 copy-done.3
  22.2 0.1 and_reduce_fusion
  22.3 0.1 or_convert_fusion
  22.4 0.5 slice_bitcast_fusion.13
  22.9 0.0 collective-permute-done.2
  22.9 2.1 collective-permute-done.3
  25.1 0.6 slice_bitcast_fusion.5
  25.7 0.0 collective-permute-done
  25.7 0.0 collective-permute-done.1
  25.7 10.6 %fusion = f32[3584]{0:T(1024)S(1)} fusion(bf16[256,4096]{1,0:T(8,128)(2,1)S(1)} %collective-permute-done.1, bf16[3072,4096]{1,0:T(8,128)(2,1)} %param.4, bf16[256,4096]{1,0:T(8,128)(2,1)} %collective-permute-done), kind=kLoop, calls=%fused_computation.1 | loop fusion | flops 117436928 | bytes 29374464 | tf_op jit(solution)/shard_map/cs,cs->c/dot_general | solution.py:38
  36.3 3.2 constant_dynamic-update-slice_fusion.1
  39.5 27.4 %constant_dynamic-update-slice_fusion = (bf16[3328,4096]{1,0:T(8,128)(2,1)}, bf16[3328,4096]{1,0:T(8,128)(2,1)}) fusion(bf16[3328,4096]{1,0:T(8,128)(2,1)} %constant_dynamic-update-slice_fusion.1, bf16[3072,4096]{1,0:T(8,128)(2,1)} %param.4), kind=kLoop, calls=%fused_computation.36 | loop fusion | bytes 75497472 | tf_op jit(solution)/shard_map/concatenate | solution.py:17
  66.8 1.5 constant_dynamic-update-slice_fusion.2
  68.4 34.1 %fusion.9 = (bf16[3072,4096]{1,0:T(8,128)(2,1)}, bf16[3072,4096]{1,0:T(8,128)(2,1)}) fusion(bf16[3328,4096]{1,0:T(8,128)(2,1)} %constant_dynamic-update-slice_fusion.2), kind=kLoop, calls=%fused_computation.57 | loop fusion | bytes 100663296 | tf_op jit(solution)/shard_map/slice | solution.py:78
  102.5 33.3 %fusion.8 = (bf16[3072,4096]{1,0:T(8,128)(2,1)}, bf16[3072,4096]{1,0:T(8,128)(2,1)}) fusion(bf16[3328,4096]{1,0:T(8,128)(2,1)} %get-tuple-element.18), kind=kLoop, calls=%fused_computation.56 | loop fusion | bytes 100663296 | tf_op jit(solution)/shard_map/slice | solution.py:78
  135.8 20.8 %multiply_reduce_fusion = (f32[24,128]{1,0:T(8,128)S(1)}, f32[24,128]{1,0:T(8,128)S(1)}) fusion(f32[24,128]{1,0:T(8,128)S(1)} %get-tuple-element.27, f32[24]{0:T(128)S(1)} %get-tuple-element.39, f32[24,128]{1,0:T(8,128)S(1)} %get-tuple-element.33, bf16[24,128,4096]{2,1,0:T(8,128)(2,1)} %bitcast.79, pred[128,128]{1,0:T(8,128)(4,1)S(1)} %iota_compare_fusion), kind=kOutput, calls=%fused_computation.17 | convolution fusion | flops 3224365056 | bytes 25231456 | tf_op jit(solution)/shard_map/tis,tjs->tij/dot_general | solution.py:43
  156.6 18.0 %fusion.2 = (f32[24,128]{1,0:T(8,128)S(1)}, f32[24,128]{1,0:T(8,128)S(1)}) fusion(f32[24,128]{1,0:T(8,128)S(1)} %get-tuple-element.26, f32[24]{0:T(128)S(1)} %get-tuple-element.38, f32[24,128]{1,0:T(8,128)S(1)} %get-tuple-element.31, f32[24,128]{1,0:T(8,128)S(1)} %get-tuple-element.33, bf16[24,128,4096]{2,1,0:T(8,128)(2,1)} %bitcast.87, ...), kind=kOutput, calls=%fused_computation.8 | convolution fusion | flops 3223971840 | bytes 50393184 | tf_op jit(solution)/shard_map/tis,tjs->tij/dot_general | solution.py:43
  174.6 18.0 %fusion.1 = (f32[24,128]{1,0:T(8,128)S(1)}, f32[24,128]{1,0:T(8,128)S(1)}) fusion(f32[24,128]{1,0:T(8,128)S(1)} %get-tuple-element.25, f32[24]{0:T(128)S(1)} %get-tuple-element.37, f32[24,128]{1,0:T(8,128)S(1)} %get-tuple-element.30, f32[24,128]{1,0:T(8,128)S(1)} %get-tuple-element.33, bf16[24,128,4096]{2,1,0:T(8,128)(2,1)} %bitcast.86, ...), kind=kOutput, calls=%fused_computation.5 | convolution fusion | flops 3223971840 | bytes 50393184 | tf_op jit(solution)/shard_map/tis,tjs->tij/dot_general | solution.py:43
  192.6 0.0 copy-start.2
  192.6 0.0 copy-start.4
  192.6 18.0 %fusion.3 = (f32[24,128]{1,0:T(8,128)S(1)}, f32[24,128]{1,0:T(8,128)S(1)}) fusion(f32[24,128]{1,0:T(8,128)S(1)} %get-tuple-element.24, f32[24]{0:T(128)S(1)} %get-tuple-element.36, f32[24,128]{1,0:T(8,128)S(1)} %get-tuple-element.29, f32[24,128]{1,0:T(8,128)S(1)} %get-tuple-element.33, bf16[24,128,4096]{2,1,0:T(8,128)(2,1)} %bitcast.85, ...), kind=kOutput, calls=%fused_computation.11 | convolution fusion | flops 3223971840 | bytes 50393184 | tf_op jit(solution)/shard_map/tis,tjs->tij/dot_general | solution.py:43
  210.6 0.0 copy-done.2
  210.6 0.0 copy-done.4
  210.7 0.0 copy-start.1
  210.7 18.2 %fusion.4 = (f32[24,128]{1,0:T(8,128)S(1)}, f32[24,128]{1,0:T(8,128)S(1)}) fusion(f32[24,128]{1,0:T(8,128)S(1)} %copy-done.2, f32[24]{0:T(128)S(1)} %copy-done.4, f32[24,128]{1,0:T(8,128)S(1)} %get-tuple-element.32, f32[24,128]{1,0:T(8,128)S(1)} %get-tuple-element.33, bf16[24,128,4096]{2,1,0:T(8,128)(2,1)} %bitcast.84, bf16[24,128,4096]{2,1,0:T(8,128)(2,1)} %bitcast.83), kind=kOutput, calls=%fused_computation.14 | convolution fusion | flops 3223971840 | bytes 50393184 | tf_op jit(solution)/shard_map/tis,tjs->tij/dot_general | solution.py:43
  228.8 0.0 copy-done.1
  228.9 0.6 fusion.7
  229.5 15.9 %convolution_bitcast_fusion = f32[4096,2]{1,0:T(8,128)} fusion(bf16[3072,4096]{1,0:T(8,128)(2,1)} %param.4, bf16[1,3072]{1,0:T(2,128)(2,1)S(1)} %stack.6), kind=kOutput, calls=%fused_computation.2 | convolution fusion | flops 50331648 | bytes 25204736
  245.4 0.0 reduce-scatter.4.cloned.1.call-update
  245.5 156.8 %reduce-scatter.4.cloned.1.call-done = f32[128,2]{1,0:T(8,128)} async-done(((f32[4096,2]{1,0:T(8,128)}), f32[128,2]{1,0:T(8,128)}) %reduce-scatter.4.cloned.1.call-update) | async-done | bytes 1040
  402.3 1.0 fusion.11
  403.2 0.1 copy.18
  403.3 0.1 copy.19
  403.4 0.6 power_bitcast_fusion
  (11 shorter events, 0.1 us)
Async XLA Ops:
  7.2 9.7 %copy-start = (bf16[3072]{0:T(1024)(128)(2,1)S(1)}, bf16[3072]{0:T(1024)(128)(2,1)}, u32[]{:S(2)}) copy-start(bf16[3072]{0:T(1024)(128)(2,1)} %param.5) | copy-start | bytes 18436
  7.2 15.0 %copy-start.5 = (s32[24]{0:T(128)S(1)}, s32[24]{0:T(128)}, u32[]{:S(2)}) copy-start(s32[24]{0:T(128)} %param.7) | copy-start | bytes 292
  7.2 15.0 %copy-start.3 = (s32[24,4]{0,1:T(4,128)S(1)}, s32[24,4]{0,1:T(4,128)}, u32[]{:S(2)}) copy-start(s32[24,4]{0,1:T(4,128)} %param.6) | copy-start | bytes 1156
  7.2 395.1 %reduce-scatter.4.cloned.1.call-start = ((), (), s32[]{:S(2)}) async-start(), calls=%async_computation.1 | async-start | bytes 2162688
  11.9 13.8 %collective-permute-start = (bf16[256,4096]{1,0:T(8,128)(2,1)}, bf16[256,4096]{1,0:T(8,128)(2,1)}, u32[]{:S(2)}, u32[]{:S(2)}) collective-permute-start(bf16[256,4096]{1,0:T(8,128)(2,1)} %get-tuple-element.20), channel_id=1, source_target_pairs={{0,1},{1,2},{2,3},{3,4},{4,5},{5,6},{6,7},{8,9},{9,10},{10,11},{11... | collective-permute-start | bytes 6291464 | tf_op jit(solution)/shard_map/ppermute | solution.py:19
  15.5 10.1 %collective-permute-start.1 = (bf16[256,4096]{1,0:T(8,128)(2,1)}, bf16[256,4096]{1,0:T(8,128)(2,1)S(1)}, u32[]{:S(2)}, u32[]{:S(2)}) collective-permute-start(bf16[256,4096]{1,0:T(8,128)(2,1)} %get-tuple-element.21), channel_id=1, source_target_pairs={{1,0},{2,1},{3,2},{4,3},{5,4},{6,5},{7,6},{9,8},{10,9},{11,10},{12... | collective-permute-start | bytes 6291464 | tf_op jit(solution)/shard_map/ppermute | solution.py:21
  16.9 6.0 %collective-permute-start.2 = (bf16[256]{0:T(256)(128)(2,1)S(1)}, bf16[256]{0:T(256)(128)(2,1)S(1)}, u32[]{:S(2)}, u32[]{:S(2)}) collective-permute-start(bf16[256]{0:T(256)(128)(2,1)S(1)} %get-tuple-element.34), channel_id=1, source_target_pairs={{0,1},{1,2},{2,3},{3,4},{4,5},{5,6},{6,7},{8,9},{9,10},{10,11},{11... | collective-permute-start | bytes 1544 | tf_op jit(solution)/shard_map/ppermute | solution.py:19
  20.8 4.3 %collective-permute-start.3 = (bf16[256]{0:T(256)(128)(2,1)S(1)}, bf16[256]{0:T(256)(128)(2,1)S(1)}, u32[]{:S(2)}, u32[]{:S(2)}) collective-permute-start(bf16[256]{0:T(256)(128)(2,1)S(1)} %get-tuple-element.35), channel_id=1, source_target_pairs={{1,0},{2,1},{3,2},{4,3},{5,4},{6,5},{7,6},{9,8},{10,9},{11,10},{12... | collective-permute-start | bytes 1544 | tf_op jit(solution)/shard_map/ppermute | solution.py:21
  192.6 18.0 %copy-start.2 = (f32[24,128]{1,0:T(8,128)S(1)}, f32[24,128]{1,0:T(8,128)}, u32[]{:S(2)}) copy-start(f32[24,128]{1,0:T(8,128)} %get-tuple-element.28) | copy-start | bytes 36868
  192.6 18.0 %copy-start.4 = (f32[24]{0:T(128)S(1)}, f32[24]{0:T(128)}, u32[]{:S(2)}) copy-start(f32[24]{0:T(128)} %get-tuple-element.40) | copy-start | bytes 292
  210.7 18.2 %copy-start.1 = (bf16[3072]{0:T(1024)(128)(2,1)S(1)}, bf16[3072]{0:T(1024)(128)(2,1)}, u32[]{:S(2)}) copy-start(bf16[3072]{0:T(1024)(128)(2,1)} %param.5) | copy-start | bytes 18436
Sparse Core Ops, SparseCore 0:
  245.6 156.6 reduce-scatter.3
where the time goes:
time: 411 us
  waiting for transfers between devices  159 us (39%)
  matrix products  109 us (27%)
  local copies, waits for them, and re-layouts  106 us (26%)
  between operations  14.3 us (3%)
  other arithmetic  12 us (3%)
  starting transfers between devices  10.2 us (2%)
    unnamed x2, waiting for transfers between devices  157 us
    dot_general x5, matrix products, tile_terms(): jnp.einsum('tis,tjs->tij', row_tiles, view_tiles, preferred_element_type=...  92.9 us
    slice x2, local copies, waits for them, and re-layouts, per_device(): ext_tiles[offset:offset + tiles_here]  67.5 us
    concatenate x2, local copies, waits for them, and re-layouts, extended_2(): jnp.concatenate([lax.ppermute(tail, axis, [(i, (i + 1) % count) for i in...  28.9 us
    unnamed x1, matrix products  15.9 us
    dot_general x1, other arithmetic, inverse_norms(): jnp.einsum('cs,cs->c', block_rows, block_rows, preferred_element_type=jnp...  10.6 us
  transfers between devices with their start and end apart: 5, of which 2 were waited for; matrix products, arithmetic and copies ran while one was open for 0% of the time, Pallas kernels for 0%

commit v1 on v0

v1 whole, which is shorter than its diff:
```python
import functools
import math

import jax
import jax.numpy as jnp
from jax import lax
from jax.experimental import pallas as pl
from jax.experimental.pallas import tpu as pltpu
from jax.sharding import PartitionSpec as P

sharpness = 40.0
epsilon = 1e-06
exponent = 0.25

TILE = 128
PAIR = 2 * TILE
SCALE = sharpness * math.log2(math.e)


def gram_dot(a, b):
    return lax.dot_general(a, b, (((1,), (1,)), ((), ())), preferred_element_type=jnp.float32)


def fold_rows(x):
    return jnp.sum(x.reshape(x.shape[0] // 8, 8, x.shape[1]), axis=0)


def main_kernel(
    n_cell, tiles, occ_hbm, cond_ref, nb_ref, cnt_ref, eff_ref, sums_ref,
    ext, gram_a, gram_b, irow, icol, crow, ccol, acc, xin, wl,
    load_sem, halo_send, halo_recv, cond_send, cond_recv, acc_send, acc_recv,
):
    rows = tiles * TILE
    pairs = tiles // 2 + 1
    last = pairs - 1
    ext_rows = rows + PAIR
    species = ext.shape[1]
    me = lax.axis_index("cell")
    first_tile = (lax.axis_index("grp") * n_cell + me) * tiles
    has_left = me > 0
    has_right = me < n_cell - 1
    left = {"cell": jnp.maximum(me - 1, 0)}
    right = {"cell": jnp.minimum(me + 1, n_cell - 1)}
    mesh_id = pl.DeviceIdType.MESH

    def load(k):
        lo, hi = max(k * PAIR, TILE), min((k + 1) * PAIR, ext_rows - TILE)
        return pltpu.make_async_copy(
            occ_hbm.at[pl.ds(lo - TILE, hi - lo)], ext.at[pl.ds(lo, hi - lo)], load_sem.at[k]
        )

    for k in list(range(1, last)) + [0, last]:
        load(k).start()

    for t in range(tiles):
        crow[t + 1] = jnp.broadcast_to(cond_ref[t : t + 1, :], (8, TILE))

    barrier = pltpu.get_barrier_semaphore()

    @pl.when(has_left)
    def _():
        pl.semaphore_signal(barrier, inc=1, device_id=left, device_id_type=mesh_id)

    @pl.when(has_right)
    def _():
        pl.semaphore_signal(barrier, inc=1, device_id=right, device_id_type=mesh_id)

    pl.semaphore_wait(barrier, has_left.astype(jnp.int32) + has_right.astype(jnp.int32))

    def remote(src, dst, send, recv, slot, target):
        return pltpu.make_async_remote_copy(
            src_ref=src, dst_ref=dst, send_sem=send.at[slot], recv_sem=recv.at[slot],
            device_id=target, device_id_type=mesh_id,
        )

    halo_r = remote(
        occ_hbm.at[pl.ds(rows - TILE, TILE)], ext.at[pl.ds(0, TILE)], halo_send, halo_recv, 0, right
    )
    halo_l = remote(
        occ_hbm.at[pl.ds(0, TILE)], ext.at[pl.ds(ext_rows - TILE, TILE)], halo_send, halo_recv, 1, left
    )
    cond_r = remote(crow.at[tiles], crow.at[0], cond_send, cond_recv, 0, right)
    cond_l = remote(crow.at[1], crow.at[tiles + 1], cond_send, cond_recv, 1, left)
    acc_r = remote(acc.at[tiles + 1], xin.at[0], acc_send, acc_recv, 0, right)
    acc_l = remote(acc.at[0], xin.at[1], acc_send, acc_recv, 1, left)

    @pl.when(has_right)
    def _():
        halo_r.start()
        cond_r.start()

    @pl.when(has_left)
    def _():
        halo_l.start()
        cond_l.start()

    @pl.when(jnp.logical_not(has_left))
    def _():
        ext[pl.ds(0, TILE), :] = jnp.zeros((TILE, species), ext.dtype)
        crow[0] = jnp.zeros((8, TILE), jnp.float32)
        xin[0] = jnp.zeros((16, TILE), jnp.float32)

    @pl.when(jnp.logical_not(has_right))
    def _():
        ext[pl.ds(ext_rows - TILE, TILE), :] = jnp.zeros((TILE, species), ext.dtype)
        crow[tiles + 1] = jnp.zeros((8, TILE), jnp.float32)
        xin[1] = jnp.zeros((16, TILE), jnp.float32)

    def column(row8):
        return jnp.transpose(jnp.broadcast_to(row8[0:1, :], (TILE, TILE)))

    for e in range(1, tiles + 1):
        ccol[e] = column(crow[e])

    def hit(t, offset):
        wanted = first_tile + t + offset
        found = jnp.int32(0)
        for s in range(nb_ref.shape[1]):
            same = jnp.logical_and(nb_ref[t, s] == wanted, s < cnt_ref[t])
            found = jnp.maximum(found, same.astype(jnp.int32))
        return found.astype(jnp.float32)

    eye = lax.broadcasted_iota(jnp.int32, (TILE, TILE), 0) == lax.broadcasted_iota(
        jnp.int32, (TILE, TILE), 1
    )

    def part(ref, base, i, j):
        return ref[base + i * TILE : base + (i + 1) * TILE, j * TILE : (j + 1) * TILE]

    def own_own(ref, base, k, near, guest=None):
        e = 2 * k
        tiles_g = [[part(ref, base, i, j) for j in range(2)] for i in range(2)]
        rows_inv = []
        cols_inv = []
        for i in range(2):
            diag = jnp.sum(jnp.where(eye, tiles_g[i][i], 0.0), axis=0, keepdims=True)
            inv = jnp.broadcast_to(lax.rsqrt(diag + epsilon), (TILE, TILE))
            col = jnp.transpose(inv) * SCALE
            irow[e + i] = inv[0:8]
            icol[e + i] = col
            rows_inv.append(inv[0:1])
            cols_inv.append(col)
        cc = [ccol[e], ccol[e + 1]]
        w = [[None, None], [None, None]]
        for i in range(2):
            for j in range(2):
                v = jnp.exp2(tiles_g[i][j] * cols_inv[i] * rows_inv[j])
                if i == j and i == guest:
                    w[i][j] = jnp.zeros_like(v)
                elif i == j:
                    w[i][j] = jnp.where(eye, 0.0, v)
                else:
                    w[i][j] = v if near is None else v * near
        for j in range(2):
            if near is None:
                numer, denom = w[j][j] * cc[j], w[j][j]
            else:
                numer, denom = w[0][j] * cc[0] + w[1][j] * cc[1], w[0][j] + w[1][j]
            acc[e + j, 0:8, :] = fold_rows(numer)
            acc[e + j, 8:16, :] = fold_rows(denom)

    def prev_own(ref, base, k, far0, near1, far1):
        e = 2 * k
        r0, r1 = irow[e, 0:1, :], irow[e + 1, 0:1, :]
        w00 = jnp.exp2(part(ref, base, 0, 0) * icol[e - 2] * r0) * far0
        w10 = jnp.exp2(part(ref, base, 1, 0) * icol[e - 1] * r0) * near1
        w11 = jnp.exp2(part(ref, base, 1, 1) * icol[e - 1] * r1) * far1
        cp0, cp1 = ccol[e - 2], ccol[e - 1]
        acc[e, 0:8, :] += fold_rows(w00 * cp0 + w10 * cp1)
        acc[e, 8:16, :] += fold_rows(w00 + w10)
        acc[e + 1, 0:8, :] += fold_rows(w11 * cp1)
        acc[e + 1, 8:16, :] += fold_rows(w11)
        c0, c1 = crow[e, 0:1, :], crow[e + 1, 0:1, :]
        acc[e - 2, 0:8, :] += fold_rows(jnp.transpose(w00 * c0))
        acc[e - 2, 8:16, :] += fold_rows(jnp.transpose(w00))
        acc[e - 1, 0:8, :] += fold_rows(jnp.transpose(w10 * c0 + w11 * c1))
        acc[e - 1, 8:16, :] += fold_rows(jnp.transpose(w10 + w11))

    def pair_rows(k, count=1):
        start = k * PAIR
        if not isinstance(k, int):
            start = pl.multiple_of(start, PAIR)
        return ext[pl.ds(start, count * PAIR), :]

    def block(k, ref):
        ref[...] = gram_dot(pair_rows(k - 1, 2), pair_rows(k))

    def block_post(k, ref):
        own_own(ref, PAIR, k, hit(2 * k - 1, 1))
        prev_own(ref, 0, k, hit(2 * k - 3, 2), hit(2 * k - 2, 1), hit(2 * k - 2, 2))

    def wait_load(k):
        start = pl.multiple_of(k * PAIR, PAIR)
        pltpu.make_async_copy(
            occ_hbm.at[pl.ds(start - TILE, PAIR)], ext.at[pl.ds(start, PAIR)], load_sem.at[k]
        ).wait()

    load(1).wait()
    gram_b[0:PAIR, :] = gram_dot(pair_rows(1), pair_rows(1))
    load(2).wait()
    block(2, gram_a)
    own_own(gram_b, 0, 1, hit(1, 1))

    def two(i, carry):
        k = 2 * i + 3
        wait_load(k)
        block(k, gram_b)
        block_post(k - 1, gram_a)
        wait_load(k + 1)
        block(k + 1, gram_a)
        block_post(k, gram_b)
        return carry

    steps = (last - 3) // 2
    lax.fori_loop(0, steps, two, 0)
    tail = 2 * steps + 3
    current = gram_a
    for k in range(tail, last):
        other = gram_b if current is gram_a else gram_a
        load(k).wait()
        block(k, other)
        block_post(k - 1, current)
        current = other

    load(0).wait()
    load(last).wait()
    other = gram_b if current is gram_a else gram_a

    @pl.when(has_left)
    def _():
        halo_r.wait_recv()
        cond_r.wait_recv()

    @pl.when(has_right)
    def _():
        halo_l.wait_recv()
        cond_l.wait_recv()

    ccol[0] = column(crow[0])
    ccol[tiles + 1] = column(crow[tiles + 1])
    other[0:PAIR, :] = gram_dot(pair_rows(0), pair_rows(0))
    other[PAIR:, :] = gram_dot(pair_rows(0), pair_rows(1))
    block_post(last - 1, current)
    block(last, current)
    own_own(other, 0, 0, hit(0, -1), 0)
    prev_own(other, PAIR, 1, hit(1, -2), hit(0, 1), hit(0, 2))
    own_own(current, PAIR, last, None, 1)
    prev_own(current, 0, last, hit(tiles - 3, 2), hit(tiles - 2, 1), hit(tiles - 2, 2))

    @pl.when(has_right)
    def _():
        acc_r.start()

    @pl.when(has_left)
    def _():
        acc_l.start()

    line = lax.broadcasted_iota(jnp.int32, (16, TILE), 0)

    def finish(t, extra):
        e = t + 1
        total = acc[e]
        if extra is not None:
            total = total + xin[extra]
        numer = jnp.sum(total[0:8], axis=0, keepdims=True)
        denom = jnp.sum(total[8:16], axis=0, keepdims=True)
        eff = crow[e, 0:1, :] * numer / denom
        eff_ref[t : t + 1, :] = eff
        both = jnp.where(line == 0, eff, jnp.where(line == 1, 1.0, 0.0))
        wl[:, t * TILE : (t + 1) * TILE] = both.astype(jnp.bfloat16)

    for t in range(1, tiles - 1):
        finish(t, None)

    step = 512 if species % 512 == 0 else TILE

    def inner(i, carry):
        cols = pl.ds(pl.multiple_of(i * step, step), step)
        got = jnp.dot(
            wl[:, TILE : rows - TILE], ext[PAIR : rows, cols], preferred_element_type=jnp.float32
        )
        sums_ref[:, cols] = got[0:8]
        return carry

    lax.fori_loop(0, species // step, inner, 0)

    @pl.when(has_left)
    def _():
        acc_r.wait_recv()

    @pl.when(has_right)
    def _():
        acc_l.wait_recv()

    finish(0, 0)
    finish(tiles - 1, 1)

    def outer(i, carry):
        cols = pl.ds(pl.multiple_of(i * step, step), step)
        got = jnp.dot(
            wl[:, 0:TILE], ext[TILE:PAIR, cols], preferred_element_type=jnp.float32
        ) + jnp.dot(
            wl[:, rows - TILE : rows], ext[rows : rows + TILE, cols],
            preferred_element_type=jnp.float32,
        )
        sums_ref[:, cols] += got[0:8]
        return carry

    lax.fori_loop(0, species // step, outer, 0)

    @pl.when(has_right)
    def _():
        halo_r.wait_send()
        cond_r.wait_send()
        acc_r.wait_send()

    @pl.when(has_left)
    def _():
        halo_l.wait_send()
        cond_l.wait_send()
        acc_l.wait_send()


def per_device(n_cell, occurrence, condition, neighbours, pair_count):
    tiles = pair_count.shape[0]
    rows, species = occurrence.shape
    cond = condition.astype(jnp.float32).reshape(tiles, TILE)
    vmem = pl.BlockSpec(memory_space=pltpu.VMEM)
    smem = pl.BlockSpec(memory_space=pltpu.SMEM)
    effective, sums = pl.pallas_call(
        functools.partial(main_kernel, n_cell, tiles),
        out_shape=(
            jax.ShapeDtypeStruct((tiles, TILE), jnp.float32),
            jax.ShapeDtypeStruct((8, species), jnp.float32),
        ),
        in_specs=[pl.BlockSpec(memory_space=pl.ANY), vmem, smem, smem],
        out_specs=(vmem, vmem),
        scratch_shapes=[
            pltpu.VMEM((rows + PAIR, species), jnp.bfloat16),
            pltpu.VMEM((2 * PAIR, PAIR), jnp.float32),
            pltpu.VMEM((2 * PAIR, PAIR), jnp.float32),
            pltpu.VMEM((tiles + 2, 8, TILE), jnp.float32),
            pltpu.VMEM((tiles + 2, TILE, TILE), jnp.float32),
            pltpu.VMEM((tiles + 2, 8, TILE), jnp.float32),
            pltpu.VMEM((tiles + 2, TILE, TILE), jnp.float32),
            pltpu.VMEM((tiles + 2, 16, TILE), jnp.float32),
            pltpu.VMEM((2, 16, TILE), jnp.float32),
            pltpu.VMEM((16, rows), jnp.bfloat16),
            pltpu.SemaphoreType.DMA((tiles // 2 + 1,)),
            pltpu.SemaphoreType.DMA((2,)),
            pltpu.SemaphoreType.DMA((2,)),
            pltpu.SemaphoreType.DMA((2,)),
            pltpu.SemaphoreType.DMA((2,)),
            pltpu.SemaphoreType.DMA((2,)),
            pltpu.SemaphoreType.DMA((2,)),
        ],
        compiler_params=pltpu.CompilerParams(
            collective_id=0, has_side_effects=True, vmem_limit_bytes=56 * 2**20
        ),
    )(occurrence, cond, neighbours, pair_count)
    totals = lax.psum_scatter(sums[0:2], ("grp", "cell"), scatter_dimension=1, tiled=True)
    persistence = (totals[0] / totals[1]) ** exponent
    return effective.reshape(rows), persistence


def solution(mesh):
    return jax.shard_map(
        functools.partial(per_device, mesh.shape["cell"]),
        mesh=mesh,
        in_specs=(
            P(("grp", "cell"), None),
            P(("grp", "cell")),
            P(("grp", "cell"), None),
            P(("grp", "cell")),
        ),
        out_specs=(P(("grp", "cell")), P(("grp", "cell"))),
        check_vma=False,
    )
```

time: 411 us -> 197 us (0.48)
  matrix products: 109 us -> 0 us
  local copies, waits for them, and re-layouts: 106 us -> 6.71 us
  Pallas kernels: 0 us -> 34.5 us
  waiting for transfers between devices: 159 us -> 140 us
  starting transfers between devices: 10.2 us -> 0.04 us
  other arithmetic: 12 us -> 1.85 us
    dot_general x5 -> x0, matrix products: 92.9 us -> none  [tile_terms(): jnp.einsum('tis,tjs->tij', row_tiles, view_tiles, preferred_element_type=...]
    slice x5 -> x1, local copies, waits for them, and re-layouts: 72.1 us -> 0.91 us  [per_device(): sums[0:2]]
    pallas_call x0 -> x1, Pallas kernels: none -> 34.5 us  [per_device(): pl.pallas_call(functools.partial(main_kernel, n_cell, tiles), out_shape=(...]
    concatenate x2 -> x0, local copies, waits for them, and re-layouts: 28.9 us -> none  [extended_2(): jnp.concatenate([lax.ppermute(tail, axis, [(i, (i + 1) % count) for i in...]
    unnamed x2, waiting for transfers between devices: 157 us -> 140 us
    unnamed x1 -> x0, matrix products: 15.9 us -> none
    dot_general x1 -> x0, other arithmetic: 10.6 us -> none  [inverse_norms(): jnp.einsum('cs,cs->c', block_rows, block_rows, preferred_element_type=jnp...]
    ppermute x4 -> x0, starting transfers between devices: 10.2 us -> none  [the longest x2 7.59 us: extended_2(): lax.ppermute(tail, axis, [(i, (i + 1) % count) for i in range(ends)])]
  transfers between devices with their start and end apart: 5 -> 1, of which waited for: 2 -> 1; matrix products, arithmetic and copies ran while one was open for 0% -> 0% of each run, Pallas kernels for 0% -> 0%
where the time goes in v1:
time: 197 us
  waiting for transfers between devices  140 us (71%)
  Pallas kernels  34.5 us (18%)
  between operations  14 us (7%)
  local copies, waits for them, and re-layouts  6.71 us (3%)
    unnamed x2, waiting for transfers between devices  140 us
    pallas_call x1, Pallas kernels, per_device(): pl.pallas_call(functools.partial(main_kernel, n_cell, tiles), out_shape=(...  34.5 us
    unnamed x5, local copies, waits for them, and re-layouts  4.8 us
  transfers between devices with their start and end apart: 1, of which 1 were waited for; matrix products, arithmetic and copies ran while one was open for 0% of the time, Pallas kernels for 0%

profile of v1, /device:TPU:0, one launch (start us, length us, event | category | flops | bytes accessed | tf_op | source)
XLA Modules:
  0.0 196.7 jit_solution(17404074712407098166)
XLA Ops:
  7.2 0.0 reduce-scatter.4.cloned.1.call-start
  7.2 1.3 bitcast_convert_fusion.cond_ref
  8.5 1.4 copy.7.nb_ref
  9.9 34.5 %shard_map.59 = (f32[24,128]{1,0:T(8,128)}, f32[8,4096]{1,0:T(8,128)}) custom-call(bf16[3072,4096]{1,0:T(8,128)(2,1)} %occ_hbm.1, f32[24,128]{1,0:T(8,128)} %bitcast_convert_fusion.cond_ref, s32[24,4]{1,0:T(8,128)} %copy.7.nb_ref, s32[24]{0:T(128)} %cnt_ref.1), custom_call_target="tpu_custom_call" | custom-call | tf_op jit(solution)/shard_map/pallas_call | solution.py:330
  44.3 0.9 slice.9
  45.2 2.0 %copy.8 = f32[2,4096]{0,1:T(8,128)} copy(f32[2,4096]{1,0:T(2,128)S(1)} %slice.9) | data formatting | bytes 65536
  47.2 0.0 reduce-scatter.4.cloned.1.call-update
  47.3 139.6 %reduce-scatter.4.cloned.1.call-done = f32[128,2]{1,0:T(8,128)} async-done(((f32[4096,2]{1,0:T(8,128)}), f32[128,2]{1,0:T(8,128)}) %reduce-scatter.4.cloned.1.call-update) | async-done | bytes 1040
  186.9 1.0 fusion
  187.9 0.1 copy.11
  187.9 0.1 copy.10
  188.0 0.6 power_bitcast_fusion
  188.6 1.3 copy.13
Async XLA Ops:
  7.2 179.7 %reduce-scatter.4.cloned.1.call-start = ((), (), s32[]{:S(2)}) async-start(), calls=%async_computation.1 | async-start | bytes 2162688
Sparse Core Ops, SparseCore 0:
  47.4 139.4 reduce-scatter.3

commit v2 on v1

--- a/solution.py
+++ b/solution.py
@@ -358,7 +358,10 @@
             collective_id=0, has_side_effects=True, vmem_limit_bytes=56 * 2**20
         ),
     )(occurrence, cond, neighbours, pair_count)
-    totals = lax.psum_scatter(sums[0:2], ("grp", "cell"), scatter_dimension=1, tiled=True)
+    axes = ("grp", "cell")
+    owners = lax.axis_size(axes)
+    blocks = jnp.transpose(sums[0:2].reshape(2, owners, species // owners), (1, 0, 2))
+    totals = jnp.sum(lax.all_to_all(blocks, axes, 0, 0, tiled=True), axis=0)
     persistence = (totals[0] / totals[1]) ** exponent
     return effective.reshape(rows), persistence
 

time: 197 us -> 56.1 us (0.28)
  waiting for transfers between devices: 140 us -> 7.24 us
  between operations: 14 us -> 0.65 us
  starting transfers between devices: 0.04 us -> 7.31 us
  local copies, waits for them, and re-layouts: 6.71 us -> 4.18 us
    unnamed x2 -> x0, waiting for transfers between devices: 140 us -> none
    all_to_all x0 -> x1, starting transfers between devices: none -> 7.31 us  [per_device(): totals = jnp.sum(lax.all_to_all(blocks, axes, 0, 0, tiled=True), axis=0)]
    all_to_all x0 -> x1, waiting for transfers between devices: none -> 7.24 us  [per_device(): totals = jnp.sum(lax.all_to_all(blocks, axes, 0, 0, tiled=True), axis=0)]
    unnamed x5 -> x2, local copies, waits for them, and re-layouts: 4.8 us -> 2.66 us
where the time goes in v2:
time: 56.1 us; the launch traced here: 55.7 us
  Pallas kernels  34.5 us (61%)
  starting transfers between devices  7.31 us (13%)
  waiting for transfers between devices  7.24 us (13%)
  local copies, waits for them, and re-layouts  4.18 us (7%)
  other arithmetic  1.87 us (3%)
  between operations  0.65 us (1%)
    pallas_call x1, Pallas kernels, per_device(): pl.pallas_call(functools.partial(main_kernel, n_cell, tiles), out_shape=(...  34.5 us
    all_to_all x1, starting transfers between devices, per_device(): totals = jnp.sum(lax.all_to_all(blocks, axes, 0, 0, tiled=True), axis=0)  7.31 us
    all_to_all x1, waiting for transfers between devices, per_device(): totals = jnp.sum(lax.all_to_all(blocks, axes, 0, 0, tiled=True), axis=0)  7.24 us
    unnamed x2, local copies, waits for them, and re-layouts  2.66 us
    transpose x1, local copies, waits for them, and re-layouts, per_device(): jnp.transpose(sums[0:2].reshape(2, owners, species // owners), (1, 0, 2))  1.52 us
    reshape x1, other arithmetic, per_device(): cond = condition.astype(jnp.float32).reshape(tiles, TILE)  1.29 us
  transfers between devices with their start and end apart: 1, of which 1 were waited for; matrix products, arithmetic and copies ran while one was open for 0% of the time, Pallas kernels for 0%

profile of v2, /device:TPU:0, one launch (start us, length us, event | category | flops | bytes accessed | tf_op | source)
XLA Modules:
  0.0 55.7 jit_solution(11316120196647287065)
XLA Ops:
  0.6 1.3 %bitcast_convert_fusion.cond_ref = f32[24,128]{1,0:T(8,128)} fusion(bf16[3072]{0:T(1024)(128)(2,1)} %param.5), kind=kLoop, calls=%fused_computation.1 | loop fusion | flops 3072 | bytes 18432 | tf_op jit(solution)/shard_map/reshape | solution.py:327
  1.9 1.4 %copy.7.nb_ref = s32[24,4]{1,0:T(8,128)} copy(s32[24,4]{0,1:T(4,128)} %param.6) | data formatting | bytes 768 | tf_op args[2]
  3.3 34.5 %shard_map.59 = (f32[24,128]{1,0:T(8,128)}, f32[8,4096]{1,0:T(8,128)}) custom-call(bf16[3072,4096]{1,0:T(8,128)(2,1)} %occ_hbm.1, f32[24,128]{1,0:T(8,128)} %bitcast_convert_fusion.cond_ref, s32[24,4]{1,0:T(8,128)} %copy.7.nb_ref, s32[24]{0:T(128)} %cnt_ref.1), custom_call_target="tpu_custom_call" | custom-call | tf_op jit(solution)/shard_map/pallas_call | solution.py:330
  37.8 1.5 %slice_bitcast_fusion = f32[32,2,128]{2,1,0:T(2,128)} fusion(f32[8,4096]{1,0:T(8,128)} %get-tuple-element.5), kind=kLoop, calls=%fused_computation | loop fusion | bytes 65536 | tf_op jit(solution)/shard_map/transpose | solution.py:363
  39.3 7.3 %all-to-all-start = ((f32[32,2,128]{2,1,0:T(2,128)}), f32[32,2,128]{2,1,0:T(2,128)S(1)}, u32[]{:S(2)}, u32[]{:S(2)}) async-start(f32[32,2,128]{2,1,0:T(2,128)} %slice_bitcast_fusion), calls=%async_computation | async-start | bytes 65536 | tf_op jit(solution)/shard_map/all_to_all | solution.py:364
  46.6 7.2 %all-to-all-done = f32[32,2,128]{2,1,0:T(2,128)S(1)} async-done(((f32[32,2,128]{2,1,0:T(2,128)}), f32[32,2,128]{2,1,0:T(2,128)S(1)}, u32[]{:S(2)}, u32[]{:S(2)}) %all-to-all-start) | async-done | bytes 32800 | tf_op jit(solution)/shard_map/all_to_all | solution.py:364
  53.9 0.5 power_bitcast_fusion
  54.4 1.3 %copy.10 = f32[3072]{0:T(1024)} copy(f32[3072]{0:T(1024)} %bitcast.10) | data formatting | bytes 24576
  (1 shorter events, 0.0 us)
Async XLA Ops:
  39.3 14.6 %all-to-all-start = ((f32[32,2,128]{2,1,0:T(2,128)}), f32[32,2,128]{2,1,0:T(2,128)S(1)}, u32[]{:S(2)}, u32[]{:S(2)}) async-start(f32[32,2,128]{2,1,0:T(2,128)} %slice_bitcast_fusion), calls=%async_computation | async-start | bytes 65536 | tf_op jit(solution)/shard_map/all_to_all | solution.py:364

commit v3 on v1

--- a/solution.py
+++ b/solution.py
@@ -321,6 +321,46 @@
         acc_l.wait_send()
 
 
+def exchange_kernel(n_cell, devices, per, wide, sums_ref, out_ref, got, send_sem, recv_sem):
+    me = lax.axis_index("grp") * n_cell + lax.axis_index("cell")
+    mesh_id = pl.DeviceIdType.MESH
+
+    def block_of(owner):
+        return sums_ref.at[:, pl.ds(pl.multiple_of((owner * per) // wide * wide, wide), wide)]
+
+    def peer(j):
+        owner = lax.rem(me + j, devices)
+        return owner, (owner // n_cell, lax.rem(owner, n_cell))
+
+    def copy(j):
+        owner, target = peer(j)
+        return pltpu.make_async_remote_copy(
+            src_ref=block_of(owner), dst_ref=got.at[j], send_sem=send_sem.at[j],
+            recv_sem=recv_sem.at[j], device_id=target, device_id_type=mesh_id,
+        )
+
+    barrier = pltpu.get_barrier_semaphore()
+
+    def greet(j, carry):
+        pl.semaphore_signal(barrier, inc=1, device_id=peer(j)[1], device_id_type=mesh_id)
+        return carry
+
+    def send(j, carry):
+        copy(j).start()
+        return carry
+
+    def finish(j, carry):
+        copy(j).wait()
+        return carry
+
+    lax.fori_loop(1, devices, greet, 0)
+    pl.semaphore_wait(barrier, devices - 1)
+    lax.fori_loop(1, devices, send, 0)
+    got[0] = block_of(me)[...]
+    lax.fori_loop(1, devices, finish, 0)
+    out_ref[...] = jnp.sum(got[...], axis=0)
+
+
 def per_device(n_cell, occurrence, condition, neighbours, pair_count):
     tiles = pair_count.shape[0]
     rows, species = occurrence.shape
@@ -358,7 +398,24 @@
             collective_id=0, has_side_effects=True, vmem_limit_bytes=56 * 2**20
         ),
     )(occurrence, cond, neighbours, pair_count)
-    totals = lax.psum_scatter(sums[0:2], ("grp", "cell"), scatter_dimension=1, tiled=True)
+    devices = lax.axis_size(("grp", "cell"))
+    per = species // devices
+    wide = max(per, TILE)
+    totals = pl.pallas_call(
+        functools.partial(exchange_kernel, n_cell, devices, per, wide),
+        out_shape=jax.ShapeDtypeStruct((8, wide), jnp.float32),
+        in_specs=[vmem],
+        out_specs=vmem,
+        scratch_shapes=[
+            pltpu.VMEM((devices, 8, wide), jnp.float32),
+            pltpu.SemaphoreType.DMA((devices,)),
+            pltpu.SemaphoreType.DMA((devices,)),
+        ],
+        compiler_params=pltpu.CompilerParams(collective_id=1, has_side_effects=True),
+    )(sums)
+    if per < wide:
+        offset = lax.rem(lax.axis_index(("grp", "cell")) * per, wide)
+        totals = lax.dynamic_slice_in_dim(totals, offset, per, axis=1)
     persistence = (totals[0] / totals[1]) ** exponent
     return effective.reshape(rows), persistence
 

time: 197 us -> 54.1 us (0.27)
  waiting for transfers between devices: 140 us -> 0 us
  between operations: 14 us -> 0.65 us
  Pallas kernels: 34.5 us -> 47.8 us
  local copies, waits for them, and re-layouts: 6.71 us -> 2.66 us
    unnamed x2 -> x0, waiting for transfers between devices: 140 us -> none
    pallas_call x0 -> x1, Pallas kernels: none -> 13.3 us  [per_device(): pl.pallas_call(functools.partial(exchange_kernel, n_cell, devices, per, w...]
    unnamed x5 -> x2, local copies, waits for them, and re-layouts: 4.8 us -> 2.66 us
  transfers between devices with their start and end apart: 1 -> 0, of which waited for: 1 -> 0; matrix products, arithmetic and copies ran while one was open for 0% -> 0% of each run, Pallas kernels for 0% -> 0%
where the time goes in v3:
time: 54.1 us; the launch traced here: 53.6 us
  Pallas kernels  47.8 us (88%)
  local copies, waits for them, and re-layouts  2.66 us (5%)
  other arithmetic  2.57 us (5%)
  between operations  0.65 us (1%)
    pallas_call x1, Pallas kernels, per_device(): pl.pallas_call(functools.partial(main_kernel, n_cell, tiles), out_shape=(...  34.5 us
    pallas_call x1, Pallas kernels, per_device(): pl.pallas_call(functools.partial(exchange_kernel, n_cell, devices, per, w...  13.3 us
    unnamed x2, local copies, waits for them, and re-layouts  2.66 us
    reshape x1, other arithmetic, per_device(): cond = condition.astype(jnp.float32).reshape(tiles, TILE)  1.29 us
    pow x1, other arithmetic, per_device(): persistence = (totals[0] / totals[1]) ** exponent  1.28 us

profile of v3, /device:TPU:0, one launch (start us, length us, event | category | flops | bytes accessed | tf_op | source)
XLA Modules:
  0.0 53.6 jit_solution(8630720883615467166)
XLA Ops:
  0.6 1.3 %bitcast_convert_fusion.cond_ref = f32[24,128]{1,0:T(8,128)} fusion(bf16[3072]{0:T(1024)(128)(2,1)} %param.5), kind=kLoop, calls=%fused_computation | loop fusion | flops 3072 | bytes 18432 | tf_op jit(solution)/shard_map/reshape | solution.py:367
  1.9 1.4 %copy.6.nb_ref = s32[24,4]{1,0:T(8,128)} copy(s32[24,4]{0,1:T(4,128)} %param.6) | data formatting | bytes 768 | tf_op args[2]
  3.3 34.5 %shard_map.59 = (f32[24,128]{1,0:T(8,128)}, f32[8,4096]{1,0:T(8,128)}) custom-call(bf16[3072,4096]{1,0:T(8,128)(2,1)} %occ_hbm.1, f32[24,128]{1,0:T(8,128)} %bitcast_convert_fusion.cond_ref, s32[24,4]{1,0:T(8,128)} %copy.6.nb_ref, s32[24]{0:T(128)} %cnt_ref.1), custom_call_target="tpu_custom_call" | custom-call | tf_op jit(solution)/shard_map/pallas_call | solution.py:370
  37.7 13.3 %shard_map.60 = f32[8,128]{1,0:T(8,128)} custom-call(f32[8,4096]{1,0:T(8,128)} %get-tuple-element.5.sums_ref), custom_call_target="tpu_custom_call" | custom-call | tf_op jit(solution)/shard_map/pallas_call | solution.py:404
  51.1 1.3 %power_bitcast_fusion = f32[128]{0:T(128)} fusion(f32[8,128]{1,0:T(8,128)} %shard_map.60), kind=kLoop, calls=%fused_computation.1 | loop fusion | flops 128 | bytes 1536 | tf_op jit(solution)/shard_map/pow | solution.py:419
  52.3 1.3 %copy.8 = f32[3072]{0:T(1024)} copy(f32[3072]{0:T(1024)} %bitcast.6) | data formatting | bytes 24576
